TPU v7x, 128 devices: a whole 4x4x4 slice. The times are simulated.
128 devices in a mesh: img: 8 (over z, y_hi), ref: 16 (over x, y_lo, core).
Axes of the slice: x: 4, y: 4 (y_hi: 2, y_lo: 2; y = y_hi * 2 + y_lo), z: 4, core: 2. Of those that a mesh axis runs over, the one named last changes fastest.
Arguments:
- images: bfloat16 [8192, 9216], P(('img', 'ref')), may hold values from -96 to 96
- references: bfloat16 [6912, 9216], P('ref'), may hold values from -0.5 to 0.5
- class_prior: float32 [192], P('ref'), may hold values from 0.2 to 5
Outputs:
- class_sums: float32 [192, 9216], P('ref', 'img')
- class_weights: float32 [192], P('ref')
All inputs are finite; a program needn't handle non-finite values.
Results may differ from a plain program's by a relative error of at most 0.0021.
Values may be sent and summed in bfloat16 or wider, within the bound.
A program may use at most 128 MiB of HBM per device.

v0:
```python
import math
import numpy as np
import jax
import jax.numpy as jnp
from jax import lax
from jax.sharding import PartitionSpec as P

ANG = 144
ROT = 36
TURN = 4


def real_dft():
    b = np.arange(ROT)
    rows = []
    for f in range(1, ROT // 2):
        rows.append(np.cos(2 * np.pi * f * b / ROT))
        rows.append(-np.sin(2 * np.pi * f * b / ROT))
    rows = [np.ones(ROT), (-1.0) ** b] + rows
    return np.array(rows).astype(np.float32)


def real_idft():
    b = np.arange(ROT)
    rows = [np.ones(ROT) / ROT, (-1.0) ** b / ROT]
    for f in range(1, ROT // 2):
        rows.append(2 * np.cos(2 * np.pi * f * b / ROT) / ROT)
        rows.append(-2 * np.sin(2 * np.pi * f * b / ROT) / ROT)
    return np.array(rows).T.astype(np.float32)


def per_device(images, references, class_prior):
    hi = lax.Precision.HIGHEST
    classes_here = class_prior.shape[0]
    n_img, pixels = images.shape
    rad = pixels // ANG
    templates = references.reshape(classes_here, ROT, pixels)[:, 0]
    half_norm = 0.5 * jnp.sum(jnp.square(templates.astype(jnp.float32)), axis=1)
    offset = jnp.log(class_prior) - half_norm
    offsets = lax.all_gather(offset, "ref", axis=0, tiled=True)
    tall = lax.all_gather(templates, "ref", axis=0, tiled=True)
    k = tall.shape[0]
    dft, idft = (real_dft(), real_idft())
    x5 = images.reshape(n_img, rad, ROT, TURN).transpose(2, 0, 1, 3).reshape(ROT, n_img, rad * TURN)
    t5 = tall.reshape(k, rad, ROT, TURN).transpose(2, 0, 1, 3).reshape(ROT, k, rad * TURN)
    xh = jnp.einsum("jb,bnc->jnc", dft, x5.astype(jnp.float32), precision=hi)
    th = jnp.einsum("jb,bkc->jkc", dft, t5.astype(jnp.float32), precision=hi)
    xr, xi = (xh[0::2], xh[1::2])
    tr, ti = (th[0::2], th[1::2])
    dot = lambda a, b: jnp.einsum("fkc,fnc->fkn", a, b, precision=hi)
    rr, ii = (dot(tr, xr), dot(ti, xi))
    ri, ir = (dot(tr[1:], xi[1:]), dot(ti[1:], xr[1:]))
    sr = jnp.concatenate([rr[:1], rr[1:] + ii[1:]])
    si = jnp.concatenate([ii[:1], ri - ir])
    sh = jnp.stack([sr, si], axis=1).reshape(ROT, k, n_img)
    scores = jnp.einsum("rj,jkn->rkn", idft, sh, precision=hi) + offsets[None, :, None]
    top = jnp.max(scores, axis=(0, 1))
    e = jnp.exp(scores - top)
    weights = (e / jnp.sum(e, axis=(0, 1))).astype(jnp.bfloat16).astype(jnp.float32)
    mass = jnp.sum(weights, axis=(0, 2))
    class_weights = lax.psum_scatter(lax.psum(mass, "img"), "ref", scatter_dimension=0, tiled=True)
    wh = jnp.einsum("jr,rkn->jkn", dft, weights, precision=hi)
    wr, wi = (wh[0::2], wh[1::2])
    dot2 = lambda a, b: jnp.einsum("fkn,fnc->fkc", a, b, precision=hi)
    cr = jnp.concatenate([dot2(wr[:1], xr[:1]), dot2(wr[1:], xr[1:]) + dot2(wi[1:], xi[1:])])
    ci = jnp.concatenate([dot2(wi[:1], xi[:1]), dot2(wr[1:], xi[1:]) - dot2(wi[1:], xr[1:])])
    c = jnp.stack([cr, ci], axis=1).reshape(ROT, k, rad, TURN)
    sums = jnp.einsum("bj,jkqc->kqbc", idft, c, precision=hi).reshape(k, pixels)
    sums = lax.psum_scatter(sums, "ref", scatter_dimension=0, tiled=True)
    class_sums = lax.psum_scatter(sums, "img", scatter_dimension=1, tiled=True)
    return (class_sums, class_weights)


def solution(mesh):
    placed = (P(("img", "ref"), None), P("ref", None), P("ref"))
    return jax.shard_map(
        per_device,
        mesh=mesh,
        in_specs=placed,
        out_specs=(P("ref", "img"), P("ref")),
        check_vma=False,
    )
```

profile of v0, /device:TPU:0, one launch (start us, length us, event | category | flops | bytes accessed | tf_op | source)
XLA Modules:
  0.0 636.5 jit_solution(5112398509001411555)
XLA Ops:
  7.2 8.7 %reshape.45 = bf16[12,36,9216]{2,1,0:T(8,128)(2,1)} reshape(bf16[432,9216]{1,0:T(8,128)(2,1)} %param.9) | data formatting | bytes 15925248 | tf_op jit(solution)/shard_map/reshape | solution.py:37
  15.9 2.5 slice.90
  18.5 2.4 copy.58
  20.9 2.9 copy.59
  23.8 3.4 copy.60
  27.3 2.5 fusion.40
  29.8 4.8 slice.75
  34.6 4.9 slice.71
  39.5 1.7 slice.96
  41.2 1.1 slice.104
  43.8 2.1 multiply_reduce_fusion
  46.0 30.8 %all-reduce = f32[192]{0:T(256)S(1)} all-reduce(f32[192]{0:T(256)S(1)} %subtract_dynamic-update-slice_fusion), channel_id=1, replica_groups=mesh['img'=8,'ref'=16] {'ref'}, use_global_device_ids=true, to_apply=%add | all-reduce | flops 192 | bytes 1536
  76.8 16.0 %copy.55 = bf16[192,1,9216]{0,2,1:T(8,128)(2,1)} copy(bf16[192,1,9216]{2,1,0:T(2,128)(2,1)} %all-gather.3.cloned.1.call-done) | data formatting | bytes 7077888 | tf_op jit(solution)/shard_map/all_gather | solution.py:41
  92.8 7.9 %reshape.46 = bf16[192,64,36,4]{0,3,2,1:T(4,128)(2,1)} reshape(bf16[192,1,9216]{0,2,1:T(8,128)(2,1)} %copy.55) | data formatting | bytes 7077888 | tf_op jit(solution)/shard_map/reshape | solution.py:45
  100.7 7.0 %copy.56 = bf16[36,192,64,4]{1,3,2,0:T(4,128)(2,1)} copy(bf16[36,192,64,4]{1,3,0,2:T(4,128)(2,1)} %bitcast.63) | data formatting | bytes 7077888 | tf_op jit(solution)/shard_map/transpose | solution.py:45
  107.7 8.5 %reshape.47 = bf16[36,192,256]{1,2,0:T(8,128)(2,1)} reshape(bf16[36,192,64,4]{1,3,2,0:T(4,128)(2,1)} %copy.56) | data formatting | bytes 7077888 | tf_op jit(solution)/shard_map/reshape | solution.py:45
  116.2 7.9 %copy.57 = bf16[36,192,256]{2,0,1:T(8,128)(2,1)} copy(bf16[36,192,256]{1,2,0:T(8,128)(2,1)} %reshape.47) | data formatting | bytes 7077888 | tf_op jit(solution)/shard_map/reshape | solution.py:45
  124.1 8.4 %fusion.39 = f32[36,192,256]{2,0,1:T(8,128)} fusion(f32[36,36,1]{1,0,2:T(8,128)S(1)} %copy-done.6, bf16[36,192,256]{2,0,1:T(8,128)(2,1)} %copy.57), kind=kOutput, calls=%fused_computation.56 | convolution fusion | flops 764411904 | bytes 10622016 | tf_op jit(solution)/shard_map/jb,bkc->jkc/dot_general | solution.py:47
  132.5 22.0 %slice.74 = f32[18,192,256]{2,0,1:T(8,128)} slice(f32[36,192,256]{2,0,1:T(8,128)} %fusion.39), slice={[1:36:2], [0:192:1], [0:256:1]} | slice | bytes 7077888 | tf_op jit(solution)/shard_map/slice | solution.py:49
  154.5 22.2 %slice.70 = f32[18,192,256]{2,0,1:T(8,128)} slice(f32[36,192,256]{2,0,1:T(8,128)} %fusion.39), slice={[0:36:2], [0:192:1], [0:256:1]} | slice | bytes 7077888 | tf_op jit(solution)/shard_map/slice | solution.py:49
  176.7 7.8 %fusion = f32[18,192,64]{1,2,0:T(8,128)S(1)} fusion(f32[18,192,256]{2,0,1:T(8,128)} %slice.74, f32[18,64,256]{2,0,1:T(8,128)} %slice.75), kind=kOutput, calls=%fused_computation.4 | convolution fusion | flops 679477248 | bytes 5603328 | tf_op jit(solution)/shard_map/fkc,fnc->fkn/dot_general | solution.py:50
  184.5 3.4 slice.97
  187.9 4.9 fusion.2
  194.0 5.1 fusion.4
  199.1 4.6 fusion.11
  204.9 4.3 add_reduce_fusion
  210.2 1.5 convert_reduce_fusion
  211.7 2.7 fusion.14
  214.4 8.1 %slice.82 = f32[18,192,64]{1,0,2:T(8,128)} slice(f32[36,192,64]{1,0,2:T(8,128)} %fusion.14), slice={[0:36:2], [0:192:1], [0:64:1]} | slice | bytes 1769472 | tf_op jit(solution)/shard_map/slice | solution.py:63
  222.5 8.1 %slice.86 = f32[18,192,64]{1,0,2:T(8,128)} slice(f32[36,192,64]{1,0,2:T(8,128)} %fusion.14), slice={[1:36:2], [0:192:1], [0:64:1]} | slice | bytes 1769472 | tf_op jit(solution)/shard_map/slice | solution.py:63
  230.6 1.7 slice.102
  232.3 1.1 slice.103
  233.5 3.4 fusion.20
  236.9 3.4 fusion.22
  240.3 3.4 convolution_subtract_fusion
  243.8 3.7 convolution_add_fusion
  248.9 3.4 pad_maximum_fusion
  252.2 14.4 %copy.84 = f32[18,2,192,256]{2,1,0,3:T(2,128)} copy(f32[18,2,192,256]{3,2,0,1:T(8,128)} %pad_maximum_fusion) | data formatting | bytes 14155776 | tf_op jit(solution)/shard_map/reshape | solution.py:67
  266.6 12.4 %reshape.69 = f32[36,192,64,4]{1,0,3,2:T(8,128)} reshape(f32[18,2,192,256]{2,1,0,3:T(2,128)} %copy.84) | data formatting | bytes 14155776 | tf_op jit(solution)/shard_map/reshape | solution.py:67
  279.0 14.2 %convolution_bitcast_fusion = f32[192,64,36,4]{0,2,3,1:T(8,128)} fusion(f32[36,192,64,4]{1,0,3,2:T(8,128)} %reshape.69, f32[36,36,1,1]{1,0,3,2:T(8,128)S(1)} %copy-done.7), kind=kOutput, calls=%fused_computation.1 | convolution fusion | flops 764411904 | bytes 14160960 | tf_op jit(solution)/shard_map/bj,jkqc->kqbc/dot_general | solution.py:68
  293.2 11.9 %copy.81 = f32[192,64,36,4]{0,3,2,1:T(4,128)} copy(f32[192,64,36,4]{0,2,3,1:T(8,128)} %convolution_bitcast_fusion) | data formatting | bytes 14155776 | tf_op jit(solution)/shard_map/bj,jkqc->kqbc/transpose | solution.py:68
  305.1 12.0 %reshape.56 = f32[192,9216]{0,1:T(8,128)} reshape(f32[192,64,36,4]{0,3,2,1:T(4,128)} %copy.81) | data formatting | bytes 14155776 | tf_op jit(solution)/shard_map/reshape | solution.py:68
  317.8 212.6 %all-reduce.5.cloned.1.call-done = f32[192,9216]{0,1:T(8,128)} async-done(((f32[192,9216]{0,1:T(8,128)}), f32[192,9216]{0,1:T(8,128)}) %all-reduce.5.cloned.1.call-update) | async-done | bytes 7077904
  530.5 6.0 constant_dynamic-slice_fusion
  536.4 29.7 %all-reduce.2 = f32[192]{0:T(256)S(1)} all-reduce(f32[192]{0:T(256)S(1)} %get-tuple-element.6), channel_id=5, replica_groups=mesh['img'=8,'ref'=16] {'ref'}, use_global_device_ids=true, to_apply=%region_7.0.clone | all-reduce | flops 192 | bytes 1536
  566.2 25.2 %psum.8 = f32[12]{0:T(128)} all-reduce(f32[12]{0:T(128)S(1)} %dynamic-slice.4), channel_id=1, replica_groups=mesh['img'=8,'ref'=16] {'img'}, use_global_device_ids=true, to_apply=%region_6.0 | all-reduce | flops 12 | bytes 96 | tf_op jit(solution)/shard_map/psum | solution.py:61
  591.4 36.2 %reduce-scatter.3.cloned.1.call-done = f32[12,1152]{0,1:T(8,128)} async-done(((f32[12,9216]{0,1:T(8,128)}), f32[12,1152]{0,1:T(8,128)}) %reduce-scatter.3.cloned.1.call-update) | async-done | bytes 55312 | tf_op jit(solution)/shard_map/reduce_scatter | solution.py:70
  627.6 1.9 copy.82
  (56 shorter events, 6.1 us)
Async XLA Ops:
  7.2 11.3 %copy-start.5 = (bf16[64,9216]{1,0:T(8,128)(2,1)S(1)}, bf16[64,9216]{1,0:T(8,128)(2,1)}, u32[]{:S(2)}) copy-start(bf16[64,9216]{1,0:T(8,128)(2,1)} %param.8) | copy-start | bytes 3538948
  7.2 69.6 %all-gather.3.cloned.1.call-start = ((), (), s32[]{:S(2)}) async-start(), calls=%async_computation.2 | async-start | bytes 7520256 | tf_op jit(solution)/shard_map/all_gather | solution.py:41
  18.4 512.0 %all-reduce.5.cloned.1.call-start = ((), (), s32[]{:S(2)}) async-start(), calls=%async_computation.3 | async-start | bytes 18874368
  23.8 3.4 copy-start.6
  39.5 2.9 copy-start
  41.2 1.3 copy-start.9
  41.2 4.7 copy-start.10
  176.7 11.2 %slice-start = ((s8[4718592]{0:T(1024)(128)(4,1)}), s8[4194304]{0:T(1024)(128)(4,1)S(1)}, s32[]{:S(2)}) async-start(s8[4718592]{0:T(1024)(128)(4,1)} %bitcast.61), calls=%async_computation.4 | async-start | bytes 8388608
  184.5 9.5 %copy-start.3 = (f32[18,192,64]{1,2,0:T(8,128)}, f32[18,192,64]{1,2,0:T(8,128)S(1)}, u32[]{:S(2)}) copy-start(f32[18,192,64]{1,2,0:T(8,128)S(1)} %fusion) | copy-start | bytes 2654212
  184.5 3.4 slice-start.1
  184.5 3.4 copy-start.1
  192.8 1.0 copy-start.4
  199.1 4.6 slice-start.2
  199.1 4.6 slice-start.3
  204.2 0.7 copy-start.8
  230.6 2.8 copy-start.2
  266.6 12.4 %copy-start.7 = (f32[36,36,1,1]{1,0,3,2:T(8,128)S(1)}, f32[36,36,1,1]{1,0,3,2:T(8,128)}, u32[]{:S(2)}) copy-start(f32[36,36,1,1]{1,0,3,2:T(8,128)} %constant.30) | copy-start | bytes 15556
  317.1 310.5 %reduce-scatter.3.cloned.1.call-start = ((), (), s32[]{:S(2)}) async-start(), calls=%async_computation.1 | async-start | bytes 5308416 | tf_op jit(solution)/shard_map/reduce_scatter | solution.py:70
Sparse Core Ops, SparseCore 0:
  18.5 48.8 all-gather.2
  317.2 213.1 all-reduce.4
  536.6 91.0 reduce-scatter.2
where the time goes:
time: 649 us; the launch traced here: 637 us
  waiting for transfers between devices  249 us (38%)
  local copies, waits for them, and re-layouts  208 us (32%)
  blocking collectives  85.7 us (13%)
  matrix products  69 us (11%)
  between operations  15.9 us (2%)
  other arithmetic  9.31 us (1%)
    unnamed x4, waiting for transfers between devices  213 us
    unnamed x2, blocking collectives  60.5 us
    slice x2, local copies, waits for them, and re-layouts, per_device(): tr, ti = (th[0::2], th[1::2])  44.2 us
    reduce_scatter x1, waiting for transfers between devices, per_device(): class_sums = lax.psum_scatter(sums, 'img', scatter_dimension=1, tiled=True)  36.2 us
    reshape x2, local copies, waits for them, and re-layouts, per_device(): c = jnp.stack([cr, ci], axis=1).reshape(ROT, k, rad, TURN)  26.8 us
    psum x1, blocking collectives, per_device(): lax.psum(mass, 'img')  25.2 us
    reshape x3, local copies, waits for them, and re-layouts, per_device(): tall.reshape(k, rad, ROT, TURN).transpose(2, 0, 1, 3)  24.3 us
    dot_general x4, matrix products, per_device(): dot = lambda a, b: jnp.einsum('fkc,fnc->fkn', a, b, precision=hi)  22.4 us
  transfers between devices with their start and end apart: 3, of which 2 were waited for; matrix products, arithmetic and copies ran while one was open for 4% of the time, Pallas kernels for 0%

commit v1 on v0

--- a/solution.py
+++ b/solution.py
@@ -4,6 +4,7 @@
 import jax.numpy as jnp
 from jax import lax
 from jax.sharding import PartitionSpec as P
+from jax.lax import all_to_all, axis_size
 
 ANG = 144
 ROT = 36
@@ -38,7 +39,15 @@
     half_norm = 0.5 * jnp.sum(jnp.square(templates.astype(jnp.float32)), axis=1)
     offset = jnp.log(class_prior) - half_norm
     offsets = lax.all_gather(offset, "ref", axis=0, tiled=True)
-    tall = lax.all_gather(templates, "ref", axis=0, tiled=True)
+    tall = jnp.concatenate(
+        all_to_all(
+            jnp.stack([templates for _ in range(axis_size("ref"))], axis=0),
+            axis_name="ref",
+            split_axis=0,
+            concat_axis=0,
+        ),
+        0,
+    )
     k = tall.shape[0]
     dft, idft = (real_dft(), real_idft())
     x5 = images.reshape(n_img, rad, ROT, TURN).transpose(2, 0, 1, 3).reshape(ROT, n_img, rad * TURN)

time: 649 us -> 741 us (1.14)
  local copies, waits for them, and re-layouts: 208 us -> 266 us
  blocking collectives: 85.7 us -> 115 us
    another operation x0 -> x2, local copies, waits for them, and re-layouts: none -> 51.1 us  [the longest x1 48.4 us: per_device(): tall.reshape(k, rad, ROT, TURN).transpose(2, 0, 1, 3)]
    all_to_all x0 -> x1, local copies, waits for them, and re-layouts: none -> 32.2 us  [per_device(): all_to_all(jnp.stack([templates for _ in range(axis_size('ref'))], axis=0...]
    unnamed x2, blocking collectives: 60.5 us -> 89.8 us
    all_gather x1 -> x0, local copies, waits for them, and re-layouts: 16 us -> none  [per_device(): tall = lax.all_gather(templates, 'ref', axis=0, tiled=True)]
    reshape x3 -> x2, local copies, waits for them, and re-layouts: 24.3 us -> 16.4 us  [per_device(): tall.reshape(k, rad, ROT, TURN).transpose(2, 0, 1, 3)]
    unnamed x4 -> x3, waiting for transfers between devices: 213 us -> 216 us
  transfers between devices with their start and end apart: 3 -> 3, of which waited for: 2 -> 2; matrix products, arithmetic and copies ran while one was open for 4% -> 3% of each run, Pallas kernels for 0% -> 0%
where the time goes in v1:
time: 741 us; the launch traced here: 731 us
  local copies, waits for them, and re-layouts  266 us (36%)
  waiting for transfers between devices  252 us (34%)
  blocking collectives  115 us (16%)
  matrix products  68.8 us (9%)
  between operations  15.9 us (2%)
  other arithmetic  7.51 us (1%)
    unnamed x3, waiting for transfers between devices  216 us
    unnamed x2, blocking collectives  89.8 us
    another operation x1, local copies, waits for them, and re-layouts, per_device(): tall.reshape(k, rad, ROT, TURN).transpose(2, 0, 1, 3)  48.4 us
    slice x2, local copies, waits for them, and re-layouts, per_device(): tr, ti = (th[0::2], th[1::2])  44.5 us
    reduce_scatter x1, waiting for transfers between devices, per_device(): class_sums = lax.psum_scatter(sums, 'img', scatter_dimension=1, tiled=True)  36.2 us
    all_to_all x1, local copies, waits for them, and re-layouts, per_device(): all_to_all(jnp.stack([templates for _ in range(axis_size('ref'))], axis=0...  32.2 us
    reshape x2, local copies, waits for them, and re-layouts, per_device(): c = jnp.stack([cr, ci], axis=1).reshape(ROT, k, rad, TURN)  26.8 us
    psum x1, blocking collectives, per_device(): lax.psum(mass, 'img')  25.2 us
  transfers between devices with their start and end apart: 3, of which 2 were waited for; matrix products, arithmetic and copies ran while one was open for 3% of the time, Pallas kernels for 0%

profile of v1, /device:TPU:0, one launch (start us, length us, event | category | flops | bytes accessed | tf_op | source)
XLA Modules:
  0.0 731.4 jit_solution(374339643918801270)
XLA Ops:
  7.2 8.6 %reshape.44 = bf16[12,36,9216]{2,1,0:T(8,128)(2,1)} reshape(bf16[432,9216]{1,0:T(8,128)(2,1)} %param.9) | data formatting | bytes 15925248 | tf_op jit(solution)/shard_map/reshape | solution.py:38
  15.8 1.7 slice.90
  17.7 2.7 stack.21
  20.4 5.7 all-to-all-start
  26.1 2.4 copy.86
  28.5 2.9 copy.87
  31.5 3.4 copy.88
  34.9 2.5 fusion.40
  37.4 4.9 slice.75
  42.3 4.9 slice.71
  47.1 1.7 slice.96
  48.8 1.1 slice.104
  51.5 60.1 %all-reduce = f32[192]{0:T(256)S(1)} all-reduce(f32[192]{0:T(256)S(1)} %subtract_dynamic-update-slice_fusion), channel_id=1, replica_groups=mesh['img'=8,'ref'=16] {'ref'}, use_global_device_ids=true, to_apply=%add | all-reduce | flops 192 | bytes 1536
  111.6 32.2 %copy.83 = bf16[16,12,9216]{1,0,2:T(8,128)(2,1)} copy(bf16[16,12,9216]{2,1,0:T(8,128)(2,1)} %all-to-all-done) | data formatting | bytes 7077888 | tf_op jit(solution)/shard_map/all_to_all | solution.py:43
  143.8 48.4 %reshape_reshape.3 = bf16[192,64,36,4]{0,3,2,1:T(4,128)(2,1)} reshape(bf16[16,12,9216]{1,0,2:T(8,128)(2,1)} %copy.83) | data formatting | bytes 7077888 | tf_op jit(solution)/shard_map/reshape;reshape | solution.py:54
  192.2 7.0 copy.84
  199.2 8.5 %reshape.45 = bf16[36,192,256]{1,2,0:T(8,128)(2,1)} reshape(bf16[36,192,64,4]{1,3,2,0:T(4,128)(2,1)} %copy.84) | data formatting | bytes 7077888 | tf_op jit(solution)/shard_map/reshape | solution.py:54
  207.7 7.9 %copy.85 = bf16[36,192,256]{2,0,1:T(8,128)(2,1)} copy(bf16[36,192,256]{1,2,0:T(8,128)(2,1)} %reshape.45) | data formatting | bytes 7077888 | tf_op jit(solution)/shard_map/reshape | solution.py:54
  215.6 8.4 %fusion.39 = f32[36,192,256]{2,0,1:T(8,128)} fusion(f32[36,36,1]{1,0,2:T(8,128)S(1)} %copy-done.6, bf16[36,192,256]{2,0,1:T(8,128)(2,1)} %copy.85), kind=kOutput, calls=%fused_computation.57 | convolution fusion | flops 764411904 | bytes 10622016 | tf_op jit(solution)/shard_map/jb,bkc->jkc/dot_general | solution.py:56
  224.0 22.0 %slice.74 = f32[18,192,256]{2,0,1:T(8,128)} slice(f32[36,192,256]{2,0,1:T(8,128)} %fusion.39), slice={[1:36:2], [0:192:1], [0:256:1]} | slice | bytes 7077888 | tf_op jit(solution)/shard_map/slice | solution.py:58
  246.0 22.5 %slice.70 = f32[18,192,256]{2,0,1:T(8,128)} slice(f32[36,192,256]{2,0,1:T(8,128)} %fusion.39), slice={[0:36:2], [0:192:1], [0:256:1]} | slice | bytes 7077888 | tf_op jit(solution)/shard_map/slice | solution.py:58
  268.5 7.8 %fusion = f32[18,192,64]{1,2,0:T(8,128)S(1)} fusion(f32[18,192,256]{2,0,1:T(8,128)} %slice.74, f32[18,64,256]{2,0,1:T(8,128)} %slice.75), kind=kOutput, calls=%fused_computation.4 | convolution fusion | flops 679477248 | bytes 5603328 | tf_op jit(solution)/shard_map/fkc,fnc->fkn/dot_general | solution.py:59
  276.3 3.4 slice.97
  279.7 4.9 fusion.2
  285.9 4.8 fusion.4
  290.6 4.6 fusion.11
  296.4 4.3 add_reduce_fusion
  301.7 1.6 convert_reduce_fusion
  303.3 2.7 fusion.14
  306.0 8.1 %slice.82 = f32[18,192,64]{1,0,2:T(8,128)} slice(f32[36,192,64]{1,0,2:T(8,128)} %fusion.14), slice={[0:36:2], [0:192:1], [0:64:1]} | slice | bytes 1769472 | tf_op jit(solution)/shard_map/slice | solution.py:72
  314.1 8.1 %slice.86 = f32[18,192,64]{1,0,2:T(8,128)} slice(f32[36,192,64]{1,0,2:T(8,128)} %fusion.14), slice={[1:36:2], [0:192:1], [0:64:1]} | slice | bytes 1769472 | tf_op jit(solution)/shard_map/slice | solution.py:72
  322.2 1.7 slice.102
  325.1 3.4 fusion.20
  328.5 3.4 fusion.22
  331.9 3.4 convolution_subtract_fusion
  335.3 3.9 convolution_add_fusion
  340.6 3.4 pad_maximum_fusion
  344.0 14.4 %copy.112 = f32[18,2,192,256]{2,1,0,3:T(2,128)} copy(f32[18,2,192,256]{3,2,0,1:T(8,128)} %pad_maximum_fusion) | data formatting | bytes 14155776 | tf_op jit(solution)/shard_map/reshape | solution.py:76
  358.4 12.4 %reshape.63 = f32[36,192,64,4]{1,0,3,2:T(8,128)} reshape(f32[18,2,192,256]{2,1,0,3:T(2,128)} %copy.112) | data formatting | bytes 14155776 | tf_op jit(solution)/shard_map/reshape | solution.py:76
  370.8 14.1 %convolution_bitcast_fusion = f32[192,64,36,4]{0,2,3,1:T(8,128)} fusion(f32[36,192,64,4]{1,0,3,2:T(8,128)} %reshape.63, f32[36,36,1,1]{1,0,3,2:T(8,128)S(1)} %copy-done.7), kind=kOutput, calls=%fused_computation.1 | convolution fusion | flops 764411904 | bytes 14160960 | tf_op jit(solution)/shard_map/bj,jkqc->kqbc/dot_general | solution.py:77
  384.9 11.9 %copy.109 = f32[192,64,36,4]{0,3,2,1:T(4,128)} copy(f32[192,64,36,4]{0,2,3,1:T(8,128)} %convolution_bitcast_fusion) | data formatting | bytes 14155776 | tf_op jit(solution)/shard_map/bj,jkqc->kqbc/transpose | solution.py:77
  396.8 12.0 %reshape.54 = f32[192,9216]{0,1:T(8,128)} reshape(f32[192,64,36,4]{0,3,2,1:T(4,128)} %copy.109) | data formatting | bytes 14155776 | tf_op jit(solution)/shard_map/reshape | solution.py:77
  409.5 215.8 %all-reduce.5.cloned.1.call-done = f32[192,9216]{0,1:T(8,128)} async-done(((f32[192,9216]{0,1:T(8,128)}), f32[192,9216]{0,1:T(8,128)}) %all-reduce.5.cloned.1.call-update) | async-done | bytes 7077904
  625.3 6.0 constant_dynamic-slice_fusion
  631.2 29.7 %all-reduce.2 = f32[192]{0:T(256)S(1)} all-reduce(f32[192]{0:T(256)S(1)} %get-tuple-element.8), channel_id=4, replica_groups=mesh['img'=8,'ref'=16] {'ref'}, use_global_device_ids=true, to_apply=%region_7.0.clone | all-reduce | flops 192 | bytes 1536
  661.0 25.2 %psum.8 = f32[12]{0:T(128)} all-reduce(f32[12]{0:T(128)S(1)} %dynamic-slice.4), channel_id=1, replica_groups=mesh['img'=8,'ref'=16] {'img'}, use_global_device_ids=true, to_apply=%region_6.0 | all-reduce | flops 12 | bytes 96 | tf_op jit(solution)/shard_map/psum | solution.py:70
  686.2 36.2 %reduce-scatter.3.cloned.1.call-done = f32[12,1152]{0,1:T(8,128)} async-done(((f32[12,9216]{0,1:T(8,128)}), f32[12,1152]{0,1:T(8,128)}) %reduce-scatter.3.cloned.1.call-update) | async-done | bytes 55312 | tf_op jit(solution)/shard_map/reduce_scatter | solution.py:79
  722.4 1.9 copy.110
  (56 shorter events, 7.3 us)
Async XLA Ops:
  20.4 5.8 copy-start.5
  20.4 91.2 %all-to-all-start = ((bf16[16,12,9216]{2,1,0:T(8,128)(2,1)}), bf16[16,12,9216]{2,1,0:T(8,128)(2,1)}, u32[]{:S(2)}, u32[]{:S(2)}) async-start(bf16[16,12,9216]{2,1,0:T(8,128)(2,1)} %stack.21), calls=%async_computation | async-start | bytes 9437184 | tf_op jit(solution)/shard_map/all_to_all | solution.py:43
  26.1 599.2 %all-reduce.5.cloned.1.call-start = ((), (), s32[]{:S(2)}) async-start(), calls=%async_computation.3 | async-start | bytes 18874368
  31.5 3.4 copy-start.6
  47.1 2.8 copy-start
  48.8 1.3 copy-start.9
  48.8 2.6 copy-start.10
  268.5 11.2 %slice-start = ((s8[4718592]{0:T(1024)(128)(4,1)}), s8[4194304]{0:T(1024)(128)(4,1)S(1)}, s32[]{:S(2)}) async-start(s8[4718592]{0:T(1024)(128)(4,1)} %bitcast.64), calls=%async_computation.4 | async-start | bytes 8388608
  276.3 9.5 %copy-start.3 = (f32[18,192,64]{1,2,0:T(8,128)}, f32[18,192,64]{1,2,0:T(8,128)S(1)}, u32[]{:S(2)}) copy-start(f32[18,192,64]{1,2,0:T(8,128)S(1)} %fusion) | copy-start | bytes 2654212
  276.3 3.4 slice-start.1
  276.3 3.4 copy-start.1
  284.6 1.0 copy-start.4
  290.6 4.6 slice-start.2
  290.6 4.6 slice-start.3
  295.7 0.7 copy-start.8
  322.2 2.8 copy-start.2
  358.4 12.4 %copy-start.7 = (f32[36,36,1,1]{1,0,3,2:T(8,128)S(1)}, f32[36,36,1,1]{1,0,3,2:T(8,128)}, u32[]{:S(2)}) copy-start(f32[36,36,1,1]{1,0,3,2:T(8,128)} %constant.30) | copy-start | bytes 15556
  408.8 313.6 %reduce-scatter.3.cloned.1.call-start = ((), (), s32[]{:S(2)}) async-start(), calls=%async_computation.2 | async-start | bytes 5308416 | tf_op jit(solution)/shard_map/reduce_scatter | solution.py:79
Sparse Core Ops, SparseCore 0:
  408.9 216.2 all-reduce.4
  631.4 91.0 reduce-scatter.2
